TPU v7x, 32 devices: a whole 2x2x4 slice. The times are simulated.
32 devices in a mesh: grp: 2 (over x), row: 16 (over z, y, core).
Axes of the slice: x: 2, y: 2, z: 4, core: 2. Of those that a mesh axis runs over, the one named last changes fastest.
Arguments:
- greens: bfloat16 [8192, 16384], P(('grp', 'row')), parts along dimension 0, may hold values from -0.0625 to 0.0625
- track_id: int32 [8192], P(('grp', 'row')), parts along dimension 0, may hold values from 0 to 7
- sigma_inv: float32 [16], P('grp'), parts along dimension 0, may hold values from 1 to 10
- sketch: float32 [192, 128, 128], P('grp', 'row'), parts along dimension 0, may hold values from -6 to 6
Outputs:
- range_basis: float32 [8192, 96], P(('grp', 'row')), parts along dimension 0
- coefficients: float32 [256, 128, 96], P(('grp', 'row')), parts along dimension 0
There are 2 independent parts, one for each index of `grp`. A program takes and returns all parts, laid end to end along the dimension named above; each array names one. Nothing has to cross between parts.
All inputs are finite; a program needn't handle non-finite values.
Results may differ from a plain program's by a relative error of at most 0.011.
Values may be sent and summed in bfloat16 or wider, within the bound.
A program may use at most 128 MiB of HBM per device.

v0:
```python
import jax
import jax.numpy as jnp
from jax import lax
from jax.sharding import PartitionSpec as P

SWEEPS = 4


smoothing = 0.24


def with_halo(x, sides, width):
    for axis, dim in sides:
        count, length = (lax.axis_size(axis), x.shape[dim])
        up = [(i, (i + 1) % count) for i in range(count - 1)]
        down = [(j, i) for i, j in up]
        last = lax.slice_in_dim(x, length - width, length, axis=dim)
        initial = lax.slice_in_dim(x, 0, width, axis=dim)
        before = lax.ppermute(last, axis, up)
        after = lax.ppermute(initial, axis, down)
        x = jnp.concatenate([before, x, after], axis=dim)
    return x


def smooth_padded(padded, field):
    padded = jnp.pad(padded, ((0, 0), (0, 0), (1, 1)))
    beside_all = (
        padded[:, 2:, 1:-1] + padded[:, :-2, 1:-1] + padded[:, 1:-1, 2:] + padded[:, 1:-1, :-2]
    )
    return field + smoothing * (beside_all - 4.0 * field)


def orthonormalize(sketched, total_rows):
    local_gram = jnp.dot(sketched.T, sketched, precision=lax.Precision.HIGHEST)
    gram_matrix = lax.psum(local_gram, "row") / total_rows
    factor = jnp.linalg.cholesky(gram_matrix)
    return lax.linalg.triangular_solve(
        factor, sketched, left_side=False, lower=True, transpose_a=True
    )


def local(greens, track_id, sigma_inv, sketch):
    local_rows = greens.shape[0]
    columns_count = sketch.shape[0]
    total_rows = local_rows * lax.axis_size("row")
    row_scale = 1.0 / jnp.sqrt(jnp.float32(total_rows))
    groups = jnp.arange(sigma_inv.shape[0], dtype=jnp.int32)
    onehot = (track_id[:, None] == groups[None, :]).astype(jnp.float32)
    weights = jnp.dot(onehot, sigma_inv, precision=lax.Precision.HIGHEST)
    field = sketch
    for sweep_index in range(SWEEPS):
        padded = with_halo(field, (("row", 1),), 1)
        field = smooth_padded(padded, field)
    omega = field.astype(jnp.bfloat16)
    portion = lax.all_gather(omega, "row", axis=1, tiled=True)
    strike = portion.shape[2]
    width = portion.shape[1] * strike
    columns = greens
    flattened = portion.reshape(portion.shape[0], width)
    first = lax.dot_general(
        columns, flattened, (((1,), (1,)), ((), ())), preferred_element_type=jnp.float32
    )
    basis_one = orthonormalize(first * weights[:, None], total_rows)
    weighted_one = (basis_one * weights[:, None]).astype(jnp.bfloat16)
    columns = greens
    back_local = lax.psum_scatter(
        lax.dot_general(
            columns, weighted_one, (((0,), (0,)), ((), ())), preferred_element_type=jnp.float32
        ),
        "row",
        scatter_dimension=0,
        tiled=True,
    )
    back_local = (back_local * row_scale).astype(jnp.bfloat16)
    columns = greens
    second = jnp.dot(
        columns,
        lax.all_gather(back_local, "row", axis=0, tiled=True),
        preferred_element_type=jnp.float32,
    )
    range_basis = orthonormalize(second * weights[:, None], total_rows)
    weighted_two = (range_basis * weights[:, None]).astype(jnp.bfloat16)
    columns = greens
    projected = lax.psum_scatter(
        lax.dot_general(
            columns, weighted_two, (((0,), (0,)), ((), ())), preferred_element_type=jnp.float32
        ),
        "row",
        scatter_dimension=0,
        tiled=True,
    )
    coefficients = (projected * row_scale).reshape(sketch.shape[1], sketch.shape[2], columns_count)
    return (range_basis, coefficients)


def solution(mesh):
    in_specs = (P(("grp", "row"), None), P(("grp", "row")), P("grp"), P("grp", "row", None))
    out_specs = (P(("grp", "row"), None), P(("grp", "row"), None, None))
    return jax.shard_map(local, mesh=mesh, in_specs=in_specs, out_specs=out_specs, check_vma=False)
```

profile of v0, /device:TPU:0, one launch (start us, length us, event | category | flops | bytes accessed | tf_op | source)
XLA Modules:
  0.0 504.1 jit_solution(15993353237637454936)
XLA Ops:
  7.2 1.2 fusion.43
  8.5 2.4 collective-permute-start.1
  10.8 1.3 collective-permute-start
  12.1 3.9 collective-permute-done
  16.1 1.9 select_maximum_fusion.6
  18.0 0.3 fusion.24
  18.4 4.7 collective-permute-start.3
  23.1 1.3 collective-permute-start.2
  24.4 1.8 collective-permute-done.2
  26.2 0.9 select_maximum_fusion.4
  27.1 0.3 fusion.20
  27.5 5.0 collective-permute-start.5
  32.5 1.3 collective-permute-start.4
  33.8 1.8 collective-permute-done.4
  35.6 0.9 select_maximum_fusion.2
  36.5 0.3 fusion.16
  36.9 5.1 %collective-permute-start.7 = (f32[96,1,128]{2,1,0:T(1,128)S(1)}, f32[96,1,128]{2,1,0:T(1,128)S(1)}, u32[]{:S(2)}, u32[]{:S(2)}) collective-permute-start(f32[96,1,128]{2,1,0:T(1,128)S(1)} %get-tuple-element.6), channel_id=1, source_target_pairs={{0,1},{1,2},{2,3},{3,4},{4,5},{5,6},{6,7},{7,8},{8,9},{9,10},{10,1... | collective-permute-start | bytes 147464 | tf_op jit(solution)/shard_map/ppermute | solution.py:19
  42.0 1.3 collective-permute-start.6
  43.3 1.8 collective-permute-done.6
  45.1 0.9 select_maximum_fusion
  46.0 1.0 fusion.12
  47.1 0.2 fusion.26
  47.3 51.2 %all-gather.3.cloned.1.call-done = bf16[96,128,128]{2,1,0:T(8,128)(2,1)} async-done(((bf16[96,8,128]{2,1,0:T(8,128)(2,1)}), bf16[96,128,128]{2,1,0:T(8,128)(2,1)}) %all-gather.3.cloned.1.call-update) | async-done | bytes 3145744 | tf_op jit(solution)/shard_map/all_gather | solution.py:55
  98.5 7.7 %fusion.5 = f32[96,256]{1,0:T(8,128)S(1)} fusion(bf16[256,16384]{1,0:T(8,128)(2,1)} %param.7, bf16[12,8,128,128]{3,2,1,0:T(8,128)(2,1)} %bitcast.61, f32[256]{0:T(256)S(1)} %bitcast.62), kind=kOutput, calls=%fused_computation.20 | convolution fusion | flops 805330944 | bytes 11633664 | tf_op jit(solution)/shard_map/dot_general | solution.py:60
  106.2 0.2 fusion.44
  106.5 59.0 %psum.14 = f32[96,96]{0,1:T(8,128)S(1)} all-reduce(f32[96,96]{0,1:T(8,128)S(1)} %fusion.44), channel_id=1, replica_groups=mesh['grp'=2,'row'=16] {'row'}, use_global_device_ids=true, to_apply=%region_0.1 | all-reduce | flops 9216 | bytes 73728 | tf_op jit(solution)/shard_map/psum | solution.py:35
  165.5 0.1 copy.7
  165.6 8.8 %cholesky.44 = f32[96,96]{1,0:T(8,128)S(1)} custom-call(f32[96,96]{1,0:T(8,128)S(1)} %fusion.35), custom_call_target="Cholesky" | custom-call | tf_op jit(solution)/shard_map/jit(cholesky)/cholesky | solution.py:36
  174.4 0.6 compare_reduce_fusion.1
  175.0 0.7 fusion.30
  175.7 7.4 %custom-call.6 = f32[1,96,96]{1,2,0:T(8,128)S(1)} custom-call(f32[1,96,96]{2,1,0:T(8,128)S(1)} %fusion.30), custom_call_target="InvertDiagBlocksLowerTriangular" | custom-call | tf_op jit(solution)/shard_map/triangular_solve/custom-call.0 | solution.py:37
  183.1 0.3 fusion.8
  183.4 7.5 %convolution_bitcast_fusion.1 = f32[16384,96]{0,1:T(8,128)} fusion(bf16[256,96]{0,1:T(8,128)(2,1)S(1)} %fusion.8, bf16[256,16384]{1,0:T(8,128)(2,1)} %param.7), kind=kOutput, calls=%fused_computation.1 | convolution fusion | flops 805306368 | bytes 14729216 | tf_op jit(solution)/shard_map/dot_general | solution.py:67
  190.9 82.5 %reduce-scatter.3.cloned.1.call-done = f32[1024,96]{0,1:T(8,128)} async-done(((f32[16384,96]{0,1:T(8,128)}), f32[1024,96]{0,1:T(8,128)}) %reduce-scatter.3.cloned.1.call-update) | async-done | bytes 393232 | tf_op jit(solution)/shard_map/reduce_scatter | solution.py:66
  273.4 1.7 multiply_convert_fusion
  275.2 45.6 %all-gather.5.cloned.1.call-done = bf16[16384,96]{0,1:T(8,128)(2,1)} async-done(((bf16[1024,96]{0,1:T(8,128)(2,1)}), bf16[16384,96]{0,1:T(8,128)(2,1)}) %all-gather.5.cloned.1.call-update) | async-done | bytes 3145744 | tf_op jit(solution)/shard_map/all_gather | solution.py:78
  320.8 7.1 %convolution_multiply_fusion = f32[96,256]{1,0:T(8,128)S(1)} fusion(bf16[16384,96]{0,1:T(8,128)(2,1)} %all-gather.5.cloned.1.call-done, bf16[256,16384]{1,0:T(8,128)(2,1)} %param.7, f32[256]{0:T(256)S(1)} %bitcast.64), kind=kOutput, calls=%fused_computation.17 | convolution fusion | flops 805330944 | bytes 11633664 | tf_op jit(solution)/shard_map/dot_general | solution.py:76
  327.9 0.2 fusion.45
  328.1 59.6 %psum.15 = f32[96,96]{0,1:T(8,128)S(1)} all-reduce(f32[96,96]{0,1:T(8,128)S(1)} %fusion.45), channel_id=1, replica_groups=mesh['grp'=2,'row'=16] {'row'}, use_global_device_ids=true, to_apply=%region_4.7 | all-reduce | flops 9216 | bytes 73728 | tf_op jit(solution)/shard_map/psum | solution.py:35
  387.7 0.1 copy.9
  387.8 8.8 %cholesky.55 = f32[96,96]{1,0:T(8,128)S(1)} custom-call(f32[96,96]{1,0:T(8,128)S(1)} %fusion.33), custom_call_target="Cholesky" | custom-call | tf_op jit(solution)/shard_map/jit(cholesky)/cholesky | solution.py:36
  396.6 0.6 compare_reduce_fusion
  397.3 0.7 fusion.31
  397.9 7.4 %custom-call.7 = f32[1,96,96]{1,2,0:T(8,128)S(1)} custom-call(f32[1,96,96]{2,1,0:T(8,128)S(1)} %fusion.31), custom_call_target="InvertDiagBlocksLowerTriangular" | custom-call | tf_op jit(solution)/shard_map/triangular_solve/custom-call.0 | solution.py:37
  405.3 0.3 convolution_bitcast_fusion.2
  405.6 7.5 %convolution_bitcast_fusion = f32[16384,96]{0,1:T(8,128)} fusion(bf16[256,16384]{1,0:T(8,128)(2,1)} %param.7, f32[256,96]{0,1:T(8,128)S(1)} %convolution_bitcast_fusion.2, f32[256]{0:T(256)S(1)} %bitcast.65), kind=kOutput, calls=%fused_computation | convolution fusion | flops 805355520 | bytes 14779392 | tf_op jit(solution)/shard_map/dot_general | solution.py:85
  413.2 82.6 %reduce-scatter.5.cloned.1.call-done = f32[1024,96]{0,1:T(8,128)} async-done(((f32[16384,96]{0,1:T(8,128)}), f32[1024,96]{0,1:T(8,128)}) %reduce-scatter.5.cloned.1.call-update) | async-done | bytes 393232 | tf_op jit(solution)/shard_map/reduce_scatter | solution.py:84
  495.8 1.8 copy_bitcast_fusion
  (29 shorter events, 0.6 us)
Async XLA Ops:
  7.2 39.9 %copy-start = (f32[8]{0:T(128)S(1)}, f32[8]{0:T(128)}, u32[]{:S(2)}) copy-start(f32[8]{0:T(128)} %param.9) | copy-start | bytes 100
  7.2 10.8 %copy-start.1 = (f32[96,8,128]{2,1,0:T(8,128)S(1)}, f32[96,8,128]{2,1,0:T(8,128)}, u32[]{:S(2)}) copy-start(f32[96,8,128]{2,1,0:T(8,128)} %param.10) | copy-start | bytes 1179652
  7.2 91.3 %all-gather.3.cloned.1.call-start = ((), (), s32[]{:S(2)}) async-start(), calls=%async_computation.2 | async-start | bytes 3342336 | tf_op jit(solution)/shard_map/all_gather | solution.py:55
  8.5 3.7 collective-permute-start.1
  10.8 5.3 %collective-permute-start = (f32[96,1,128]{2,1,0:T(1,128)S(1)}, f32[96,1,128]{2,1,0:T(1,128)S(1)}, u32[]{:S(2)}, u32[]{:S(2)}) collective-permute-start(f32[96,1,128]{2,1,0:T(1,128)S(1)} %get-tuple-element.13), channel_id=1, source_target_pairs={{1,0},{2,1},{3,2},{4,3},{5,4},{6,5},{7,6},{8,7},{9,8},{10,9},{11,1... | collective-permute-start | bytes 147464 | tf_op jit(solution)/shard_map/ppermute | solution.py:20
  18.4 6.0 %collective-permute-start.3 = (f32[96,1,128]{2,1,0:T(1,128)S(1)}, f32[96,1,128]{2,1,0:T(1,128)S(1)}, u32[]{:S(2)}, u32[]{:S(2)}) collective-permute-start(f32[96,1,128]{2,1,0:T(1,128)S(1)} %get-tuple-element.10), channel_id=1, source_target_pairs={{0,1},{1,2},{2,3},{3,4},{4,5},{5,6},{6,7},{7,8},{8,9},{9,10},{10,1... | collective-permute-start | bytes 147464 | tf_op jit(solution)/shard_map/ppermute | solution.py:19
  23.1 3.1 collective-permute-start.2
  27.5 6.3 %collective-permute-start.5 = (f32[96,1,128]{2,1,0:T(1,128)S(1)}, f32[96,1,128]{2,1,0:T(1,128)S(1)}, u32[]{:S(2)}, u32[]{:S(2)}) collective-permute-start(f32[96,1,128]{2,1,0:T(1,128)S(1)} %get-tuple-element.8), channel_id=1, source_target_pairs={{0,1},{1,2},{2,3},{3,4},{4,5},{5,6},{6,7},{7,8},{8,9},{9,10},{10,1... | collective-permute-start | bytes 147464 | tf_op jit(solution)/shard_map/ppermute | solution.py:19
  32.5 3.1 collective-permute-start.4
  36.9 6.4 %collective-permute-start.7 = (f32[96,1,128]{2,1,0:T(1,128)S(1)}, f32[96,1,128]{2,1,0:T(1,128)S(1)}, u32[]{:S(2)}, u32[]{:S(2)}) collective-permute-start(f32[96,1,128]{2,1,0:T(1,128)S(1)} %get-tuple-element.6), channel_id=1, source_target_pairs={{0,1},{1,2},{2,3},{3,4},{4,5},{5,6},{6,7},{7,8},{8,9},{9,10},{10,1... | collective-permute-start | bytes 147464 | tf_op jit(solution)/shard_map/ppermute | solution.py:19
  42.0 5.1 %copy-start.3 = (s32[256]{0:T(256)S(1)}, s32[256]{0:T(256)}, u32[]{:S(2)}) copy-start(s32[256]{0:T(256)} %param.8) | copy-start | bytes 3076
  42.0 3.1 collective-permute-start.6
  47.1 226.4 %reduce-scatter.3.cloned.1.call-start = ((), (), s32[]{:S(2)}) async-start(), calls=%async_computation.3 | async-start | bytes 6684672 | tf_op jit(solution)/shard_map/reduce_scatter | solution.py:66
  190.9 129.9 %all-gather.5.cloned.1.call-start = ((), (), s32[]{:S(2)}) async-start(), calls=%async_computation.4 | async-start | bytes 3342336 | tf_op jit(solution)/shard_map/all_gather | solution.py:78
  275.2 220.6 %reduce-scatter.5.cloned.1.call-start = ((), (), s32[]{:S(2)}) async-start(), calls=%async_computation.5 | async-start | bytes 6684672 | tf_op jit(solution)/shard_map/reduce_scatter | solution.py:84
  405.6 7.5 %copy-start.2 = (f32[256,96]{0,1:T(8,128)}, f32[256,96]{0,1:T(8,128)S(1)}, u32[]{:S(2)}) copy-start(f32[256,96]{0,1:T(8,128)S(1)} %convolution_bitcast_fusion.2) | copy-start | bytes 294916
Sparse Core Ops, SparseCore 0:
  47.2 51.2 all-gather.2
  191.0 82.3 reduce-scatter.2
  276.4 44.3 all-gather.4
  413.3 82.4 reduce-scatter.4
where the time goes:
time: 505 us; the launch traced here: 504 us
  waiting for transfers between devices  271 us (54%)
  blocking collectives  119 us (24%)
  other arithmetic  44.9 us (9%)
  matrix products  31 us (6%)
  starting transfers between devices  22.5 us (4%)
  between operations  14.1 us (3%)
    psum x2, blocking collectives, orthonormalize(): gram_matrix = lax.psum(local_gram, 'row') / total_rows  119 us
    reduce_scatter x1, waiting for transfers between devices, local(): lax.psum_scatter(lax.dot_general(columns, weighted_two, (((0,), (0,)), ((...  82.6 us
    reduce_scatter x1, waiting for transfers between devices, local(): lax.psum_scatter(lax.dot_general(columns, weighted_one, (((0,), (0,)), ((...  82.5 us
    all_gather x1, waiting for transfers between devices, local(): portion = lax.all_gather(omega, 'row', axis=1, tiled=True)  51.2 us
    all_gather x1, waiting for transfers between devices, local(): lax.all_gather(back_local, 'row', axis=0, tiled=True)  45.6 us
    another operation x6, other arithmetic, orthonormalize(): factor = jnp.linalg.cholesky(gram_matrix)  18.9 us
    ppermute x4, starting transfers between devices, with_halo(): before = lax.ppermute(last, axis, up)  17.1 us
    another operation x4, other arithmetic, orthonormalize(): lax.linalg.triangular_solve(factor, sketched, left_side=False, lower=True...  16 us
  transfers between devices with their start and end apart: 12, of which 8 were waited for; matrix products, arithmetic and copies ran while one was open for 0% of the time, Pallas kernels for 0%

commit v1 on v0

v1 whole, which is shorter than its diff:
```python
import functools
import jax
import jax.numpy as jnp
from jax import lax
from jax.experimental import pallas as pl
from jax.experimental.pallas import tpu as pltpu
from jax.sharding import PartitionSpec as P

SWEEPS = 4
smoothing = 0.24
VMEM_LIMIT = 52 * 1024 * 1024


def smooth(sketch):
    length = sketch.shape[1]
    count = lax.axis_size("row")
    before, after = [], []
    for hop in range(1, -(-SWEEPS // length) + 1):
        take = min(length, SWEEPS - (hop - 1) * length)
        up = [(i, i + hop) for i in range(count - hop)]
        down = [(j, i) for i, j in up]
        before.insert(0, lax.ppermute(sketch[:, length - take :], "row", up))
        after.append(lax.ppermute(sketch[:, :take], "row", down))
    field = jnp.concatenate(before + [sketch] + after, axis=1)
    first_row = lax.axis_index("row") * length - SWEEPS
    for sweep in range(1, SWEEPS + 1):
        padded = jnp.pad(field, ((0, 0), (0, 0), (1, 1)))
        centre = field[:, 1:-1]
        beside_all = (
            padded[:, 2:, 1:-1] + padded[:, :-2, 1:-1] + padded[:, 1:-1, 2:] + padded[:, 1:-1, :-2]
        )
        field = centre + smoothing * (beside_all - 4.0 * centre)
        if sweep < SWEEPS:
            rows = first_row + sweep + jnp.arange(field.shape[1], dtype=jnp.int32)
            inside = (rows >= 0) & (rows < length * count)
            field = jnp.where(inside[None, :, None], field, 0.0)
    return field


class Place:
    def __init__(self, n):
        self.n = n
        self.steps = n.bit_length() - 1
        self.me = lax.axis_index("row")
        rest = list(range(1, self.steps))
        self.orders = ([0] + rest, [0] + rest[1:] + rest[:1])

    def bit(self, k, of=None):
        return lax.rem(lax.div(self.me if of is None else of, 2**k), 2)

    def partner(self, k):
        return {"row": self.me + 2**k * (1 - 2 * self.bit(k))}

    def slot(self, block, order):
        return sum(self.bit(k, block) * 2 ** (self.steps - 1 - i) for i, k in enumerate(order))

    def greet(self):
        barrier = pltpu.get_barrier_semaphore()
        for k in range(self.steps):
            pl.semaphore_signal(
                barrier, inc=1, device_id=self.partner(k), device_id_type=pl.DeviceIdType.MESH
            )
        pl.semaphore_wait(barrier, self.steps)

    def send(self, source, target, k, sems, *at):
        copy = pltpu.make_async_remote_copy(
            src_ref=source,
            dst_ref=target,
            send_sem=sems.at[(0, *at)],
            recv_sem=sems.at[(1, *at)],
            device_id=self.partner(k),
            device_id_type=pl.DeviceIdType.MESH,
        )
        copy.start()
        return copy


def reduce_scatter(place, g_ref, w_ref, acc, wide, outgo, income, sems):
    n, depth = place.n, acc[0].shape[1]
    width = acc[0].shape[2]
    own = place.bit(0)

    def produce(core):
        def body(j, carry):
            block = 2 * j + core
            columns = pl.ds(pl.multiple_of(block * width, 128), width)
            part = jnp.dot(w_ref[...], g_ref[:, columns], preferred_element_type=jnp.float32)
            for s in range(2):
                acc[s][place.slot(block, place.orders[s])] = part[s * depth : (s + 1) * depth]
            return carry

        lax.fori_loop(0, n // 2, body, 0)

    produce(1 - own)
    half = n // 2
    copies = [
        place.send(acc[s].at[pl.ds((1 - own) * half, half)], wide[s], 0, sems, 0, s)
        for s in range(2)
    ]
    produce(own)
    base = [own * half, own * half]
    arrived, arrived_at, at = wide, 0, 0
    for step in range(1, place.steps):
        half = n >> (step + 1)
        for s in range(2):
            k = place.orders[s][step]
            mine = place.bit(k)
            copies[s].wait()

            def pack(i, carry):
                j = (1 - mine) * half + i
                total = acc[s][base[s] + j] + arrived[s][arrived_at + j].astype(jnp.float32)
                outgo[s][at + i] = total.astype(jnp.bfloat16)
                return carry

            def keep(i, carry):
                j = mine * half + i
                acc[s][base[s] + j] += arrived[s][arrived_at + j].astype(jnp.float32)
                return carry

            lax.fori_loop(0, half, pack, 0)
            copies[s] = place.send(
                outgo[s].at[pl.ds(at, half)], income[s].at[pl.ds(at, half)], k, sems, step, s
            )
            lax.fori_loop(0, half, keep, 0)
            base[s] = base[s] + mine * half
        arrived, arrived_at, at = income, at, at + half
    results = []
    for s in range(2):
        copies[s].wait()
        results.append(acc[s][base[s]] + arrived[s][arrived_at].astype(jnp.float32))
    return results


def gather_product(place, g_ref, held, total, sems):
    n, depth, width = place.n, held[0].shape[1], held[0].shape[2]

    def multiply(s, start, count):
        order = place.orders[s]

        def body(i, carry):
            slot = start + i
            block = sum(
                lax.rem(lax.div(slot, 2 ** (place.steps - 1 - i)), 2) * 2**k
                for i, k in enumerate(order)
            )
            columns = pl.ds(pl.multiple_of(block * width, 128), width)
            total[s * depth : (s + 1) * depth, :] += lax.dot_general(
                held[s][slot],
                g_ref[:, columns],
                (((1,), (1,)), ((), ())),
                preferred_element_type=jnp.float32,
            )
            return carry

        lax.fori_loop(0, count, body, 0)

    total[...] = jnp.zeros_like(total)
    base = [place.slot(place.me, place.orders[s]) for s in range(2)]
    fresh = list(base)
    count = 1
    for step in reversed(range(place.steps)):
        half = n >> (step + 1)
        copies = []
        for s in range(2):
            region = held[s].at[pl.ds(base[s], half)]
            copies.append(place.send(region, region, place.orders[s][step], sems, step, s))
        for s in range(2):
            multiply(s, fresh[s], count)
        for s in range(2):
            copies[s].wait()
            mine = place.bit(place.orders[s][step])
            fresh[s] = base[s] + (1 - 2 * mine) * half
            base[s] = base[s] - mine * half
        count = half
    for s in range(2):
        multiply(s, fresh[s], count)


def gram_total(place, y, sums, income, sems):
    sums[0] = lax.dot_general(
        y, y, (((1,), (1,)), ((), ())),
        precision=lax.Precision.HIGHEST, preferred_element_type=jnp.float32,
    )
    for k in range(place.steps):
        place.send(sums.at[k], income.at[k], k, sems, k).wait()
        sums[k + 1] = sums[k] + income[k]
    return sums[place.steps]


def finish(place, weights_ref, y_ref, gram_ref, total, sums, income, sems):
    y_ref[...] = total[...] * weights_ref[...]
    gram_ref[...] = gram_total(place, y_ref[...], sums, income, sems)


def first_kernel(n, g_ref, omega_ref, weights_ref, y_ref, gram_ref, h0, h1, total, sums, gin, ag_sems, gram_sems):
    place = Place(n)
    depth = h0.shape[1]
    for s, held in enumerate((h0, h1)):
        held[place.slot(place.me, place.orders[s])] = omega_ref[s * depth : (s + 1) * depth]
    place.greet()
    gather_product(place, g_ref, (h0, h1), total, ag_sems)
    finish(place, weights_ref, y_ref, gram_ref, total, sums, gin, gram_sems)


def second_kernel(n, scale, g_ref, w_ref, weights_ref, y_ref, gram_ref,
                  a0, a1, f0, f1, o0, o1, i0, i1, rs_sems,
                  h0, h1, total, sums, gin, ag_sems, gram_sems):
    place = Place(n)
    place.greet()
    results = reduce_scatter(place, g_ref, w_ref, (a0, a1), (f0, f1), (o0, o1), (i0, i1), rs_sems)
    for s, held in enumerate((h0, h1)):
        held[place.slot(place.me, place.orders[s])] = (results[s] * scale).astype(jnp.bfloat16)
    gather_product(place, g_ref, (h0, h1), total, ag_sems)
    finish(place, weights_ref, y_ref, gram_ref, total, sums, gin, gram_sems)


def last_kernel(n, scale, g_ref, w_ref, out_ref, a0, a1, f0, f1, o0, o1, i0, i1, rs_sems):
    place = Place(n)
    depth = a0.shape[1]
    place.greet()
    results = reduce_scatter(place, g_ref, w_ref, (a0, a1), (f0, f1), (o0, o1), (i0, i1), rs_sems)
    for s in range(2):
        out_ref[s * depth : (s + 1) * depth] = results[s] * scale


def local(greens, track_id, sigma_inv, sketch):
    rows, params = greens.shape
    columns = sketch.shape[0]
    n = lax.axis_size("row")
    steps = n.bit_length() - 1
    width, depth = params // n, columns // 2
    total_rows = rows * n
    scale = 1.0 / float(total_rows) ** 0.5
    groups = jnp.arange(sigma_inv.shape[0], dtype=jnp.int32)
    onehot = (track_id[:, None] == groups[None, :]).astype(jnp.float32)
    weights = jnp.dot(onehot, sigma_inv, precision=lax.Precision.HIGHEST)[None, :]
    f32, bf16 = jnp.float32, jnp.bfloat16

    scatter_scratch = (
        [pltpu.VMEM((n, depth, width), f32)] * 2
        + [pltpu.VMEM((n // 2, depth, width), f32)] * 2
        + [pltpu.VMEM((n // 2, depth, width), bf16)] * 4
        + [pltpu.SemaphoreType.DMA((2, steps, 2))]
    )
    gather_scratch = [pltpu.VMEM((n, depth, width), bf16)] * 2 + [
        pltpu.VMEM((columns, rows), f32),
        pltpu.VMEM((steps + 1, columns, columns), f32),
        pltpu.VMEM((steps, columns, columns), f32),
        pltpu.SemaphoreType.DMA((2, steps, 2)),
        pltpu.SemaphoreType.DMA((2, steps)),
    ]
    vmem = pl.BlockSpec(memory_space=pltpu.VMEM)
    flops = 2 * rows * params * columns
    product_shapes = (
        jax.ShapeDtypeStruct((columns, rows), f32),
        jax.ShapeDtypeStruct((columns, columns), f32),
    )

    def call(kernel, number, shapes, scratch, *operands):
        return pl.pallas_call(
            kernel,
            out_shape=shapes,
            in_specs=[vmem] * len(operands),
            out_specs=jax.tree.map(lambda _: vmem, shapes),
            scratch_shapes=scratch,
            cost_estimate=pl.CostEstimate(
                flops=flops, bytes_accessed=2 * rows * params, transcendentals=0
            ),
            compiler_params=pltpu.CompilerParams(
                collective_id=number, has_side_effects=True, vmem_limit_bytes=VMEM_LIMIT
            ),
        )(*operands)

    def orthonormal(sketched, gram):
        factor = jnp.linalg.cholesky(gram / total_rows)
        return lax.linalg.triangular_solve(factor, sketched, left_side=True, lower=True)

    omega = smooth(sketch).astype(bf16).reshape(columns, width)
    first, gram = call(
        functools.partial(first_kernel, n), 0, product_shapes, gather_scratch, greens, omega, weights
    )
    weighted_one = (orthonormal(first, gram) * weights).astype(bf16)
    second, gram = call(
        functools.partial(second_kernel, n, scale), 1, product_shapes,
        scatter_scratch + gather_scratch, greens, weighted_one, weights,
    )
    basis = orthonormal(second, gram)
    weighted_two = (basis * weights).astype(bf16)
    projected = call(
        functools.partial(last_kernel, n, scale), 2,
        jax.ShapeDtypeStruct((columns, width), f32), scatter_scratch, greens, weighted_two,
    )
    coefficients = projected.reshape(sketch.shape).transpose(1, 2, 0)
    return (basis.T, coefficients)


def solution(mesh):
    in_specs = (P(("grp", "row"), None), P(("grp", "row")), P("grp"), P("grp", "row", None))
    out_specs = (P(("grp", "row"), None), P(("grp", "row"), None, None))
    return jax.shard_map(local, mesh=mesh, in_specs=in_specs, out_specs=out_specs, check_vma=False)
```

time: 505 us -> 228 us (0.45)
  waiting for transfers between devices: 271 us -> 3.22 us
  Pallas kernels: 0 us -> 178 us
  blocking collectives: 119 us -> 0 us
  matrix products: 31 us -> 2.09 us
  starting transfers between devices: 22.5 us -> 3.66 us
  between operations: 14.1 us -> 0.87 us
  other arithmetic: 44.9 us -> 37.9 us
    pallas_call x0 -> x3, Pallas kernels: none -> 178 us  [call(): pl.pallas_call(kernel, out_shape=shapes, in_specs=[vmem] * len(operands),...]
    reduce_scatter x2 -> x0, waiting for transfers between devices: 165 us -> none  [the longest x1 82.6 us: local(): lax.psum_scatter(lax.dot_general(columns, weighted_two, (((0,), (0,)), ((...]
    psum x2 -> x0, blocking collectives: 119 us -> none  [orthonormalize(): gram_matrix = lax.psum(local_gram, 'row') / total_rows]
    all_gather x2 -> x0, waiting for transfers between devices: 96.8 us -> none  [the longest x1 51.2 us: local(): portion = lax.all_gather(omega, 'row', axis=1, tiled=True)]
    dot_general x7 -> x1, matrix products: 30.5 us -> 0.87 us  [local(): jnp.dot(onehot, sigma_inv, precision=lax.Precision.HIGHEST)[None, :]]
    ppermute x8 -> x2, starting transfers between devices: 22.3 us -> 3.66 us  [the longest x1 2.37 us: smooth(): before.insert(0, lax.ppermute(sketch[:, length - take:], 'row', up))]
    ppermute x8 -> x2, waiting for transfers between devices: 9.4 us -> 3.22 us  [the longest x1 3.22 us: smooth(): after.append(lax.ppermute(sketch[:, :take], 'row', down))]
  transfers between devices with their start and end apart: 12 -> 2, of which waited for: 8 -> 1; matrix products, arithmetic and copies ran while one was open for 0% -> 0% of each run, Pallas kernels for 0% -> 0%
where the time goes in v1:
time: 228 us
  Pallas kernels  178 us (78%)
  other arithmetic  37.9 us (17%)
  starting transfers between devices  3.66 us (2%)
  waiting for transfers between devices  3.22 us (1%)
  local copies, waits for them, and re-layouts  2.37 us (1%)
    pallas_call x3, Pallas kernels, call(): pl.pallas_call(kernel, out_shape=shapes, in_specs=[vmem] * len(operands),...  178 us
    another operation x6, other arithmetic, orthonormal(): factor = jnp.linalg.cholesky(gram / total_rows)  18.9 us
    another operation x4, other arithmetic, orthonormal(): lax.linalg.triangular_solve(factor, sketched, left_side=True, lower=True)  16 us
  transfers between devices with their start and end apart: 2, of which 1 were waited for; matrix products, arithmetic and copies ran while one was open for 0% of the time, Pallas kernels for 0%

profile of v1, /device:TPU:0, one launch (start us, length us, event | category | flops | bytes accessed | tf_op | source)
XLA Modules:
  0.0 227.8 jit_solution(13228097955728872852)
XLA Ops:
  0.6 0.0 copy-start
  0.6 1.2 fusion.37
  1.9 2.4 %collective-permute-start = (f32[96,4,128]{2,1,0:T(4,128)S(1)}, f32[96,4,128]{2,1,0:T(4,128)S(1)}, u32[]{:S(2)}, u32[]{:S(2)}) collective-permute-start(f32[96,4,128]{2,1,0:T(4,128)S(1)} %get-tuple-element.12), channel_id=1, source_target_pairs={{0,1},{1,2},{2,3},{3,4},{4,5},{5,6},{6,7},{7,8},{8,9},{9,10},{10,1... | collective-permute-start | bytes 589832 | tf_op jit(solution)/shard_map/ppermute | solution.py:22
  4.3 1.3 collective-permute-start.1
  5.6 0.0 copy-done
  5.6 0.9 fusion.25.weights_ref
  6.5 0.0 collective-permute-done
  6.5 3.2 %collective-permute-done.1 = f32[96,4,128]{2,1,0:T(4,128)S(1)} collective-permute-done((f32[96,4,128]{2,1,0:T(4,128)S(1)}, f32[96,4,128]{2,1,0:T(4,128)S(1)}, u32[]{:S(2)}, u32[]{:S(2)}) %collective-permute-start.1) | collective-permute-done | bytes 196640 | tf_op jit(solution)/shard_map/ppermute | solution.py:23
  9.7 1.1 pad_maximum_fusion
  10.9 0.5 fusion.6
  11.4 0.5 fusion.12
  11.9 0.5 fusion.18
  12.4 0.3 fusion.24
  12.7 55.4 %shard_map.59 = (f32[96,256]{1,0:T(8,128)S(1)}, f32[96,96]{1,0:T(8,128)S(1)}) custom-call(bf16[256,16384]{1,0:T(8,128)(2,1)} %g_ref.5, bf16[96,1024]{1,0:T(8,128)(2,1)S(1)} %bitcast.38, f32[1,256]{1,0:T(1,128)S(1)} %fusion.25.weights_ref), custom_call_target="tpu_custom_call" | custom-call | flops 805306368 | bytes 8388608 | tf_op jit(solution)/shard_map/pallas_call | solution.py:261
  68.0 0.1 copy.6
  68.1 0.1 copy.7
  68.3 8.8 %cholesky.44 = f32[96,96]{1,0:T(8,128)S(1)} custom-call(f32[96,96]{1,0:T(8,128)S(1)} %fusion.33), custom_call_target="Cholesky" | custom-call | tf_op jit(solution)/shard_map/jit(cholesky)/cholesky | solution.py:276
  77.1 0.6 compare_reduce_fusion.1
  77.7 0.7 fusion.27
  78.4 7.4 %custom-call.6 = f32[1,96,96]{1,2,0:T(8,128)S(1)} custom-call(f32[1,96,96]{2,1,0:T(8,128)S(1)} %fusion.27), custom_call_target="InvertDiagBlocksLowerTriangular" | custom-call | tf_op jit(solution)/shard_map/triangular_solve/custom-call.0 | solution.py:277
  85.7 0.3 fusion.w_ref
  86.0 81.9 %shard_map.60 = (f32[96,256]{1,0:T(8,128)S(1)}, f32[96,96]{1,0:T(8,128)S(1)}) custom-call(bf16[256,16384]{1,0:T(8,128)(2,1)} %g_ref.5, bf16[96,256]{1,0:T(8,128)(2,1)S(1)} %fusion.w_ref, f32[1,256]{1,0:T(1,128)S(1)} %fusion.25.weights_ref), custom_call_target="tpu_custom_call" | custom-call | flops 805306368 | bytes 8388608 | tf_op jit(solution)/shard_map/pallas_call | solution.py:261
  167.9 0.1 copy.8
  168.0 0.1 copy.9
  168.1 8.8 %cholesky.55 = f32[96,96]{1,0:T(8,128)S(1)} custom-call(f32[96,96]{1,0:T(8,128)S(1)} %fusion.31), custom_call_target="Cholesky" | custom-call | tf_op jit(solution)/shard_map/jit(cholesky)/cholesky | solution.py:276
  176.9 0.6 compare_reduce_fusion
  177.6 0.7 fusion.28
  178.2 7.4 %custom-call.7 = f32[1,96,96]{1,2,0:T(8,128)S(1)} custom-call(f32[1,96,96]{2,1,0:T(8,128)S(1)} %fusion.28), custom_call_target="InvertDiagBlocksLowerTriangular" | custom-call | tf_op jit(solution)/shard_map/triangular_solve/custom-call.0 | solution.py:277
  185.6 0.9 multiply_convert_fusion
  186.5 40.5 %shard_map.61 = f32[96,1024]{1,0:T(8,128)S(1)} custom-call(bf16[256,16384]{1,0:T(8,128)(2,1)} %g_ref.5, bf16[96,256]{1,0:T(8,128)(2,1)S(1)} %get-tuple-element.14.w_ref), custom_call_target="tpu_custom_call" | custom-call | flops 805306368 | bytes 8388608 | tf_op jit(solution)/shard_map/pallas_call | solution.py:261
  227.1 0.8 bitcast_bitcast_fusion
  (10 shorter events, 0.2 us)
Async XLA Ops:
  0.6 5.0 %copy-start = (f32[8]{0:T(128)S(1)}, f32[8]{0:T(128)}, u32[]{:S(2)}) copy-start(f32[8]{0:T(128)} %param.9) | copy-start | bytes 100
  1.9 4.6 %collective-permute-start = (f32[96,4,128]{2,1,0:T(4,128)S(1)}, f32[96,4,128]{2,1,0:T(4,128)S(1)}, u32[]{:S(2)}, u32[]{:S(2)}) collective-permute-start(f32[96,4,128]{2,1,0:T(4,128)S(1)} %get-tuple-element.12), channel_id=1, source_target_pairs={{0,1},{1,2},{2,3},{3,4},{4,5},{5,6},{6,7},{7,8},{8,9},{9,10},{10,1... | collective-permute-start | bytes 589832 | tf_op jit(solution)/shard_map/ppermute | solution.py:22
  4.3 5.5 %collective-permute-start.1 = (f32[96,4,128]{2,1,0:T(4,128)S(1)}, f32[96,4,128]{2,1,0:T(4,128)S(1)}, u32[]{:S(2)}, u32[]{:S(2)}) collective-permute-start(f32[96,4,128]{2,1,0:T(4,128)S(1)} %get-tuple-element.13), channel_id=1, source_target_pairs={{1,0},{2,1},{3,2},{4,3},{5,4},{6,5},{7,6},{8,7},{9,8},{10,9},{11,1... | collective-permute-start | bytes 589832 | tf_op jit(solution)/shard_map/ppermute | solution.py:23

commit v2 on v1

--- a/solution.py
+++ b/solution.py
@@ -75,55 +75,114 @@
         return copy
 
 
-def reduce_scatter(place, g_ref, w_ref, acc, wide, outgo, income, sems):
+def fetch(g_hbm, g_ref, loads, width):
+    def copy(block):
+        columns = pl.ds(pl.multiple_of(block * width, 128), width)
+        return pltpu.make_async_copy(g_hbm.at[:, columns], g_ref.at[:, columns], loads.at[block])
+
+    return copy
+
+
+def quarters(place):
+    a, b = place.bit(1), place.bit(2)
+    return ((1 - a, 1 - b), (1 - a, b), (a, 1 - b), (a, b))
+
+
+def over_blocks(place, core, quarter, visit):
+    first = core + 2 * quarter[0] + 4 * quarter[1]
+
+    def body(j, carry):
+        visit(8 * j + first)
+        return carry
+
+    lax.fori_loop(0, place.n // 8, body, 0)
+
+
+def start_loads(place, load):
+    own = place.bit(0)
+    for core in (1 - own, own):
+        for quarter in quarters(place):
+            over_blocks(place, core, quarter, lambda block: load(block).start())
+
+
+def reduce_scatter(place, load, g_ref, w_ref, acc, wide, outgo, income, sems):
     n, depth = place.n, acc[0].shape[1]
     width = acc[0].shape[2]
     own = place.bit(0)
-
-    def produce(core):
-        def body(j, carry):
-            block = 2 * j + core
+    parts = quarters(place)
+    fourth = n // 4
+
+    def produce(core, quarter):
+        def visit(block):
+            load(block).wait()
             columns = pl.ds(pl.multiple_of(block * width, 128), width)
             part = jnp.dot(w_ref[...], g_ref[:, columns], preferred_element_type=jnp.float32)
             for s in range(2):
                 acc[s][place.slot(block, place.orders[s])] = part[s * depth : (s + 1) * depth]
-            return carry
-
-        lax.fori_loop(0, n // 2, body, 0)
-
-    produce(1 - own)
-    half = n // 2
-    copies = [
-        place.send(acc[s].at[pl.ds((1 - own) * half, half)], wide[s], 0, sems, 0, s)
-        for s in range(2)
-    ]
-    produce(own)
-    base = [own * half, own * half]
+
+        over_blocks(place, core, quarter, visit)
+
+    def across(s, piece):
+        mine = place.bit(place.orders[s][1])
+        at = (1 - mine if piece == 0 else mine) * fourth
+        return place.send(
+            acc[s].at[pl.ds((1 - own) * (n // 2) + at, fourth)],
+            wide[s].at[pl.ds(at, fourth)], 0, sems, place.steps if piece else 0, s,
+        )
+
+    pieces = [[None, None], [None, None]]
+    produce(1 - own, parts[0])
+    produce(1 - own, parts[1])
+    pieces[0][0] = across(0, 0)
+    produce(1 - own, parts[2])
+    pieces[1][0] = across(1, 0)
+    produce(1 - own, parts[3])
+    pieces[0][1] = across(0, 1)
+    pieces[1][1] = across(1, 1)
+    produce(own, parts[0])
+    produce(own, parts[1])
+
+    base = [own * (n // 2), own * (n // 2)]
+    copies = [None, None]
     arrived, arrived_at, at = wide, 0, 0
     for step in range(1, place.steps):
         half = n >> (step + 1)
-        for s in range(2):
+
+        def add(s, offset, target, target_at):
+            def body(i, carry):
+                j = offset + i
+                sum_ = acc[s][base[s] + j] + arrived[s][arrived_at + j].astype(jnp.float32)
+                target[s][target_at + i] = sum_.astype(target[s].dtype)
+                return carry
+
+            lax.fori_loop(0, half, body, 0)
+
+        def out(s):
+            (pieces[s][0] if step == 1 else copies[s]).wait()
             k = place.orders[s][step]
-            mine = place.bit(k)
-            copies[s].wait()
-
-            def pack(i, carry):
-                j = (1 - mine) * half + i
-                total = acc[s][base[s] + j] + arrived[s][arrived_at + j].astype(jnp.float32)
-                outgo[s][at + i] = total.astype(jnp.bfloat16)
-                return carry
-
-            def keep(i, carry):
-                j = mine * half + i
-                acc[s][base[s] + j] += arrived[s][arrived_at + j].astype(jnp.float32)
-                return carry
-
-            lax.fori_loop(0, half, pack, 0)
+            add(s, (1 - place.bit(k)) * half, outgo, at)
             copies[s] = place.send(
                 outgo[s].at[pl.ds(at, half)], income[s].at[pl.ds(at, half)], k, sems, step, s
             )
-            lax.fori_loop(0, half, keep, 0)
+
+        def keep(s):
+            mine = place.bit(place.orders[s][step])
+            if step == 1:
+                pieces[s][1].wait()
+            add(s, mine * half, acc, base[s] + mine * half)
             base[s] = base[s] + mine * half
+
+        if step == 1:
+            out(0)
+            produce(own, parts[2])
+            out(1)
+            produce(own, parts[3])
+            keep(0)
+            keep(1)
+        else:
+            for s in range(2):
+                out(s)
+                keep(s)
         arrived, arrived_at, at = income, at, at + half
     results = []
     for s in range(2):
@@ -132,8 +191,9 @@
     return results
 
 
-def gather_product(place, g_ref, held, total, sems):
+def gather_product(place, g_ref, held, total, sems, ready=None):
     n, depth, width = place.n, held[0].shape[1], held[0].shape[2]
+    over = (1 - 2 * place.bit(0)) * (n // 2)
 
     def multiply(s, start, count):
         order = place.orders[s]
@@ -155,26 +215,41 @@
 
         lax.fori_loop(0, count, body, 0)
 
+    def forward(s, step):
+        region = held[s].at[pl.ds(fresh[s], count)]
+        return place.send(region, region, 0, sems, place.steps + step, s)
+
     total[...] = jnp.zeros_like(total)
     base = [place.slot(place.me, place.orders[s]) for s in range(2)]
     fresh = list(base)
     count = 1
-    for step in reversed(range(place.steps)):
+    for step in reversed(range(1, place.steps)):
         half = n >> (step + 1)
         copies = []
         for s in range(2):
             region = held[s].at[pl.ds(base[s], half)]
             copies.append(place.send(region, region, place.orders[s][step], sems, step, s))
+        across = [forward(s, step) for s in range(2)]
+        if ready is not None:
+            ready()
+            ready = None
         for s in range(2):
             multiply(s, fresh[s], count)
+        for s in range(2):
+            across[s].wait()
+            multiply(s, fresh[s] + over, count)
         for s in range(2):
             copies[s].wait()
             mine = place.bit(place.orders[s][step])
             fresh[s] = base[s] + (1 - 2 * mine) * half
             base[s] = base[s] - mine * half
         count = half
+    across = [forward(s, 0) for s in range(2)]
     for s in range(2):
         multiply(s, fresh[s], count)
+    for s in range(2):
+        across[s].wait()
+        multiply(s, fresh[s] + over, count)
 
 
 def gram_total(place, y, sums, income, sems):
@@ -193,33 +268,47 @@
     gram_ref[...] = gram_total(place, y_ref[...], sums, income, sems)
 
 
-def first_kernel(n, g_ref, omega_ref, weights_ref, y_ref, gram_ref, h0, h1, total, sums, gin, ag_sems, gram_sems):
+def first_kernel(n, g_hbm, omega_ref, weights_ref, y_ref, gram_ref, g_ref, loads, h0, h1, total, sums, gin, ag_sems, gram_sems):
     place = Place(n)
-    depth = h0.shape[1]
+    depth, width = h0.shape[1:]
+    load = fetch(g_hbm, g_ref, loads, width)
+    start_loads(place, load)
+
+    def ready():
+        def body(block, carry):
+            load(block).wait()
+            return carry
+
+        lax.fori_loop(0, n, body, 0)
+
     for s, held in enumerate((h0, h1)):
         held[place.slot(place.me, place.orders[s])] = omega_ref[s * depth : (s + 1) * depth]
     place.greet()
-    gather_product(place, g_ref, (h0, h1), total, ag_sems)
+    gather_product(place, g_ref, (h0, h1), total, ag_sems, ready)
     finish(place, weights_ref, y_ref, gram_ref, total, sums, gin, gram_sems)
 
 
-def second_kernel(n, scale, g_ref, w_ref, weights_ref, y_ref, gram_ref,
+def second_kernel(n, scale, g_hbm, w_ref, weights_ref, y_ref, gram_ref, g_ref, loads,
                   a0, a1, f0, f1, o0, o1, i0, i1, rs_sems,
                   h0, h1, total, sums, gin, ag_sems, gram_sems):
     place = Place(n)
+    load = fetch(g_hbm, g_ref, loads, a0.shape[2])
+    start_loads(place, load)
     place.greet()
-    results = reduce_scatter(place, g_ref, w_ref, (a0, a1), (f0, f1), (o0, o1), (i0, i1), rs_sems)
+    results = reduce_scatter(place, load, g_ref, w_ref, (a0, a1), (f0, f1), (o0, o1), (i0, i1), rs_sems)
     for s, held in enumerate((h0, h1)):
         held[place.slot(place.me, place.orders[s])] = (results[s] * scale).astype(jnp.bfloat16)
     gather_product(place, g_ref, (h0, h1), total, ag_sems)
     finish(place, weights_ref, y_ref, gram_ref, total, sums, gin, gram_sems)
 
 
-def last_kernel(n, scale, g_ref, w_ref, out_ref, a0, a1, f0, f1, o0, o1, i0, i1, rs_sems):
+def last_kernel(n, scale, g_hbm, w_ref, out_ref, g_ref, loads, a0, a1, f0, f1, o0, o1, i0, i1, rs_sems):
     place = Place(n)
-    depth = a0.shape[1]
+    depth, width = a0.shape[1:]
+    load = fetch(g_hbm, g_ref, loads, width)
+    start_loads(place, load)
     place.greet()
-    results = reduce_scatter(place, g_ref, w_ref, (a0, a1), (f0, f1), (o0, o1), (i0, i1), rs_sems)
+    results = reduce_scatter(place, load, g_ref, w_ref, (a0, a1), (f0, f1), (o0, o1), (i0, i1), rs_sems)
     for s in range(2):
         out_ref[s * depth : (s + 1) * depth] = results[s] * scale
 
@@ -241,13 +330,13 @@
         [pltpu.VMEM((n, depth, width), f32)] * 2
         + [pltpu.VMEM((n // 2, depth, width), f32)] * 2
         + [pltpu.VMEM((n // 2, depth, width), bf16)] * 4
-        + [pltpu.SemaphoreType.DMA((2, steps, 2))]
+        + [pltpu.SemaphoreType.DMA((2, steps + 1, 2))]
     )
     gather_scratch = [pltpu.VMEM((n, depth, width), bf16)] * 2 + [
         pltpu.VMEM((columns, rows), f32),
         pltpu.VMEM((steps + 1, columns, columns), f32),
         pltpu.VMEM((steps, columns, columns), f32),
-        pltpu.SemaphoreType.DMA((2, steps, 2)),
+        pltpu.SemaphoreType.DMA((2, 2 * steps, 2)),
         pltpu.SemaphoreType.DMA((2, steps)),
     ]
     vmem = pl.BlockSpec(memory_space=pltpu.VMEM)
@@ -261,9 +350,9 @@
         return pl.pallas_call(
             kernel,
             out_shape=shapes,
-            in_specs=[vmem] * len(operands),
+            in_specs=[pl.BlockSpec(memory_space=pl.ANY)] + [vmem] * (len(operands) - 1),
             out_specs=jax.tree.map(lambda _: vmem, shapes),
-            scratch_shapes=scratch,
+            scratch_shapes=[pltpu.VMEM((rows, params), bf16), pltpu.SemaphoreType.DMA((n,))] + scratch,
             cost_estimate=pl.CostEstimate(
                 flops=flops, bytes_accessed=2 * rows * params, transcendentals=0
             ),

time: 228 us -> 207 us (0.908)
  Pallas kernels: 178 us -> 157 us
    pallas_call x3, Pallas kernels: 178 us -> 157 us  [call(): pl.pallas_call(kernel, out_shape=shapes, in_specs=[pl.BlockSpec(memory_sp...]
where the time goes in v2:
time: 207 us
  Pallas kernels  157 us (76%)
  other arithmetic  37.9 us (18%)
  starting transfers between devices  3.66 us (2%)
  waiting for transfers between devices  3.22 us (2%)
  local copies, waits for them, and re-layouts  2.37 us (1%)
  matrix products  2.09 us (1%)
    pallas_call x3, Pallas kernels, call(): pl.pallas_call(kernel, out_shape=shapes, in_specs=[pl.BlockSpec(memory_sp...  157 us
    another operation x6, other arithmetic, orthonormal(): factor = jnp.linalg.cholesky(gram / total_rows)  18.9 us
    another operation x4, other arithmetic, orthonormal(): lax.linalg.triangular_solve(factor, sketched, left_side=True, lower=True)  16 us
  transfers between devices with their start and end apart: 2, of which 1 were waited for; matrix products, arithmetic and copies ran while one was open for 0% of the time, Pallas kernels for 0%

profile of v2, /device:TPU:0, one launch (start us, length us, event | category | flops | bytes accessed | tf_op | source)
XLA Modules:
  0.0 207.1 jit_solution(9386088608115684466)
XLA Ops:
  0.6 0.0 copy-start
  0.6 1.2 fusion.37
  1.9 2.4 %collective-permute-start = (f32[96,4,128]{2,1,0:T(4,128)S(1)}, f32[96,4,128]{2,1,0:T(4,128)S(1)}, u32[]{:S(2)}, u32[]{:S(2)}) collective-permute-start(f32[96,4,128]{2,1,0:T(4,128)S(1)} %get-tuple-element.12), channel_id=1, source_target_pairs={{0,1},{1,2},{2,3},{3,4},{4,5},{5,6},{6,7},{7,8},{8,9},{9,10},{10,1... | collective-permute-start | bytes 589832 | tf_op jit(solution)/shard_map/ppermute | solution.py:22
  4.3 1.3 collective-permute-start.1
  5.6 0.0 copy-done
  5.6 0.9 fusion.25.weights_ref
  6.5 0.0 collective-permute-done
  6.5 3.2 %collective-permute-done.1 = f32[96,4,128]{2,1,0:T(4,128)S(1)} collective-permute-done((f32[96,4,128]{2,1,0:T(4,128)S(1)}, f32[96,4,128]{2,1,0:T(4,128)S(1)}, u32[]{:S(2)}, u32[]{:S(2)}) %collective-permute-start.1) | collective-permute-done | bytes 196640 | tf_op jit(solution)/shard_map/ppermute | solution.py:23
  9.7 1.1 pad_maximum_fusion
  10.9 0.5 fusion.6
  11.4 0.5 fusion.12
  11.9 0.5 fusion.18
  12.4 0.3 fusion.24
  12.7 49.3 %shard_map.59 = (f32[96,256]{1,0:T(8,128)S(1)}, f32[96,96]{1,0:T(8,128)S(1)}) custom-call(bf16[256,16384]{1,0:T(8,128)(2,1)} %g_hbm.5, bf16[96,1024]{1,0:T(8,128)(2,1)S(1)} %bitcast.38, f32[1,256]{1,0:T(1,128)S(1)} %fusion.25.weights_ref), custom_call_target="tpu_custom_call" | custom-call | flops 805306368 | bytes 8388608 | tf_op jit(solution)/shard_map/pallas_call | solution.py:350
  62.0 0.1 copy.6
  62.1 0.1 copy.7
  62.2 8.8 %cholesky.44 = f32[96,96]{1,0:T(8,128)S(1)} custom-call(f32[96,96]{1,0:T(8,128)S(1)} %fusion.33), custom_call_target="Cholesky" | custom-call | tf_op jit(solution)/shard_map/jit(cholesky)/cholesky | solution.py:365
  71.0 0.6 compare_reduce_fusion.1
  71.7 0.7 fusion.27
  72.3 7.4 %custom-call.6 = f32[1,96,96]{1,2,0:T(8,128)S(1)} custom-call(f32[1,96,96]{2,1,0:T(8,128)S(1)} %fusion.27), custom_call_target="InvertDiagBlocksLowerTriangular" | custom-call | tf_op jit(solution)/shard_map/triangular_solve/custom-call.0 | solution.py:366
  79.7 0.3 fusion.w_ref
  80.0 74.0 %shard_map.60 = (f32[96,256]{1,0:T(8,128)S(1)}, f32[96,96]{1,0:T(8,128)S(1)}) custom-call(bf16[256,16384]{1,0:T(8,128)(2,1)} %g_hbm.5, bf16[96,256]{1,0:T(8,128)(2,1)S(1)} %fusion.w_ref, f32[1,256]{1,0:T(1,128)S(1)} %fusion.25.weights_ref), custom_call_target="tpu_custom_call" | custom-call | flops 805306368 | bytes 8388608 | tf_op jit(solution)/shard_map/pallas_call | solution.py:350
  154.0 0.1 copy.8
  154.1 0.1 copy.9
  154.2 8.8 %cholesky.55 = f32[96,96]{1,0:T(8,128)S(1)} custom-call(f32[96,96]{1,0:T(8,128)S(1)} %fusion.31), custom_call_target="Cholesky" | custom-call | tf_op jit(solution)/shard_map/jit(cholesky)/cholesky | solution.py:365
  163.0 0.6 compare_reduce_fusion
  163.7 0.7 fusion.28
  164.3 7.4 %custom-call.7 = f32[1,96,96]{1,2,0:T(8,128)S(1)} custom-call(f32[1,96,96]{2,1,0:T(8,128)S(1)} %fusion.28), custom_call_target="InvertDiagBlocksLowerTriangular" | custom-call | tf_op jit(solution)/shard_map/triangular_solve/custom-call.0 | solution.py:366
  171.7 0.9 multiply_convert_fusion
  172.6 33.7 %shard_map.61 = f32[96,1024]{1,0:T(8,128)S(1)} custom-call(bf16[256,16384]{1,0:T(8,128)(2,1)} %g_hbm.5, bf16[96,256]{1,0:T(8,128)(2,1)S(1)} %get-tuple-element.14.w_ref), custom_call_target="tpu_custom_call" | custom-call | flops 805306368 | bytes 8388608 | tf_op jit(solution)/shard_map/pallas_call | solution.py:350
  206.3 0.8 bitcast_bitcast_fusion
  (10 shorter events, 0.2 us)
Async XLA Ops:
  0.6 5.0 %copy-start = (f32[8]{0:T(128)S(1)}, f32[8]{0:T(128)}, u32[]{:S(2)}) copy-start(f32[8]{0:T(128)} %param.9) | copy-start | bytes 100
  1.9 4.6 %collective-permute-start = (f32[96,4,128]{2,1,0:T(4,128)S(1)}, f32[96,4,128]{2,1,0:T(4,128)S(1)}, u32[]{:S(2)}, u32[]{:S(2)}) collective-permute-start(f32[96,4,128]{2,1,0:T(4,128)S(1)} %get-tuple-element.12), channel_id=1, source_target_pairs={{0,1},{1,2},{2,3},{3,4},{4,5},{5,6},{6,7},{7,8},{8,9},{9,10},{10,1... | collective-permute-start | bytes 589832 | tf_op jit(solution)/shard_map/ppermute | solution.py:22
  4.3 5.5 %collective-permute-start.1 = (f32[96,4,128]{2,1,0:T(4,128)S(1)}, f32[96,4,128]{2,1,0:T(4,128)S(1)}, u32[]{:S(2)}, u32[]{:S(2)}) collective-permute-start(f32[96,4,128]{2,1,0:T(4,128)S(1)} %get-tuple-element.13), channel_id=1, source_target_pairs={{1,0},{2,1},{3,2},{4,3},{5,4},{6,5},{7,6},{8,7},{9,8},{10,9},{11,1... | collective-permute-start | bytes 589832 | tf_op jit(solution)/shard_map/ppermute | solution.py:23

commit v3 on v2

--- a/solution.py
+++ b/solution.py
@@ -313,6 +313,33 @@
         out_ref[s * depth : (s + 1) * depth] = results[s] * scale
 
 
+def orthonormal_kernel(total_rows, gram_ref, y_ref, weights_ref, basis_ref, weighted_ref, inverse):
+    size = gram_ref.shape[0]
+    lane = lax.broadcasted_iota(jnp.int32, (1, size), 1)
+    below = lax.broadcasted_iota(jnp.int32, (8, 1), 0)
+    groups = [gram_ref[i : i + 8] / total_rows for i in range(0, size, 8)]
+    for k in range(size):
+        own, place = k // 8, k % 8
+        row = groups[own][place : place + 1]
+        pivot = row[:, k : k + 1]
+        row = jnp.where(lane == k, 1.0, row)
+        inverse[k : k + 1] = jnp.where(lane <= k, row, 0.0) * lax.rsqrt(pivot)
+        row = row / pivot
+        for g in range(own, size // 8):
+            column = groups[g][:, k : k + 1]
+            cleared = jnp.where(lane == k, 0.0, groups[g])
+            if g == own:
+                groups[g] = jnp.where(below > place, cleared - column * row, groups[g])
+            else:
+                groups[g] = cleared - column * row
+    basis = jnp.dot(
+        inverse[...], y_ref[...],
+        precision=lax.Precision.HIGHEST, preferred_element_type=jnp.float32,
+    )
+    basis_ref[...] = basis
+    weighted_ref[...] = (basis * weights_ref[...]).astype(jnp.bfloat16)
+
+
 def local(greens, track_id, sigma_inv, sketch):
     rows, params = greens.shape
     columns = sketch.shape[0]
@@ -362,20 +389,27 @@
         )(*operands)
 
     def orthonormal(sketched, gram):
-        factor = jnp.linalg.cholesky(gram / total_rows)
-        return lax.linalg.triangular_solve(factor, sketched, left_side=True, lower=True)
+        return pl.pallas_call(
+            functools.partial(orthonormal_kernel, float(total_rows)),
+            out_shape=(
+                jax.ShapeDtypeStruct((columns, rows), f32),
+                jax.ShapeDtypeStruct((columns, rows), bf16),
+            ),
+            in_specs=[vmem] * 3,
+            out_specs=(vmem, vmem),
+            scratch_shapes=[pltpu.VMEM((columns, columns), f32)],
+        )(gram, sketched, weights)
 
     omega = smooth(sketch).astype(bf16).reshape(columns, width)
     first, gram = call(
         functools.partial(first_kernel, n), 0, product_shapes, gather_scratch, greens, omega, weights
     )
-    weighted_one = (orthonormal(first, gram) * weights).astype(bf16)
+    _, weighted_one = orthonormal(first, gram)
     second, gram = call(
         functools.partial(second_kernel, n, scale), 1, product_shapes,
         scatter_scratch + gather_scratch, greens, weighted_one, weights,
     )
-    basis = orthonormal(second, gram)
-    weighted_two = (basis * weights).astype(bf16)
+    basis, weighted_two = orthonormal(second, gram)
     projected = call(
         functools.partial(last_kernel, n, scale), 2,
         jax.ShapeDtypeStruct((columns, width), f32), scatter_scratch, greens, weighted_two,

time: 207 us -> 195 us (0.942)
  other arithmetic: 37.9 us -> 2.91 us
  Pallas kernels: 157 us -> 176 us
  local copies, waits for them, and re-layouts: 2.37 us -> 6.78 us
    another operation x10 -> x0, other arithmetic: 34.9 us -> none  [the longest x6 18.9 us: orthonormal(): factor = jnp.linalg.cholesky(gram / total_rows)]
    pallas_call x0 -> x2, Pallas kernels: none -> 19.7 us  [orthonormal(): pl.pallas_call(functools.partial(orthonormal_kernel, float(total_rows)),...]
    unnamed x3 -> x19, local copies, waits for them, and re-layouts: 0.04 us -> 4.77 us
where the time goes in v3:
time: 195 us
  Pallas kernels  176 us (90%)
  local copies, waits for them, and re-layouts  6.78 us (3%)
  starting transfers between devices  3.66 us (2%)
  waiting for transfers between devices  3.19 us (2%)
  other arithmetic  2.91 us (1%)
    pallas_call x3, Pallas kernels, call(): pl.pallas_call(kernel, out_shape=shapes, in_specs=[pl.BlockSpec(memory_sp...  157 us
    pallas_call x2, Pallas kernels, orthonormal(): pl.pallas_call(functools.partial(orthonormal_kernel, float(total_rows)),...  19.7 us
    unnamed x19, local copies, waits for them, and re-layouts  4.77 us
  transfers between devices with their start and end apart: 2, of which 1 were waited for; matrix products, arithmetic and copies ran while one was open for 0% of the time, Pallas kernels for 0%

profile of v3, /device:TPU:0, one launch (start us, length us, event | category | flops | bytes accessed | tf_op | source)
XLA Modules:
  0.0 194.7 jit_solution(10231165015284815683)
XLA Ops:
  0.6 0.0 copy-start
  0.6 1.2 fusion.27
  1.9 2.4 %collective-permute-start = (f32[96,4,128]{2,1,0:T(4,128)S(1)}, f32[96,4,128]{2,1,0:T(4,128)S(1)}, u32[]{:S(2)}, u32[]{:S(2)}) collective-permute-start(f32[96,4,128]{2,1,0:T(4,128)S(1)} %get-tuple-element.16), channel_id=1, source_target_pairs={{0,1},{1,2},{2,3},{3,4},{4,5},{5,6},{6,7},{7,8},{8,9},{9,10},{10,1... | collective-permute-start | bytes 589832 | tf_op jit(solution)/shard_map/ppermute | solution.py:22
  4.3 1.3 collective-permute-start.1
  5.6 0.0 copy-done
  5.6 0.9 fusion.24.weights_ref
  6.5 0.0 copy-start.7
  6.5 0.0 collective-permute-done
  6.6 3.2 %collective-permute-done.1 = f32[96,4,128]{2,1,0:T(4,128)S(1)} collective-permute-done((f32[96,4,128]{2,1,0:T(4,128)S(1)}, f32[96,4,128]{2,1,0:T(4,128)S(1)}, u32[]{:S(2)}, u32[]{:S(2)}) %collective-permute-start.1) | collective-permute-done | bytes 196640 | tf_op jit(solution)/shard_map/ppermute | solution.py:23
  9.7 1.1 pad_maximum_fusion
  10.9 0.5 fusion.5
  11.4 0.5 fusion.11
  11.9 0.5 fusion.17
  12.4 0.3 fusion.23
  12.7 0.0 copy-done.7
  12.7 49.5 %shard_map.59 = (f32[96,256]{1,0:T(8,128)S(1)}, f32[96,96]{1,0:T(8,128)S(1)}) custom-call(bf16[256,16384]{1,0:T(8,128)(2,1)} %g_hbm.5, bf16[96,1024]{1,0:T(8,128)(2,1)S(1)} %bitcast.16, f32[1,256]{1,0:T(1,128)S(1)} %fusion.24.weights_ref), custom_call_target="tpu_custom_call" | custom-call | flops 805306368 | bytes 8388608 | tf_op jit(solution)/shard_map/pallas_call | solution.py:377
  62.2 0.0 copy-start.2
  62.2 0.6 copy-done.2
  62.9 0.0 copy-start.6
  62.9 0.6 copy-done.6
  63.5 9.8 %shard_map.60 = (f32[96,256]{1,0:T(8,128)}, bf16[96,256]{1,0:T(8,128)(2,1)}) custom-call(f32[96,96]{1,0:T(8,128)} %copy-done.6, f32[96,256]{1,0:T(8,128)} %copy-done.2, f32[1,256]{1,0:T(1,128)} %copy-done.7), custom_call_target="tpu_custom_call" | custom-call | tf_op jit(solution)/shard_map/pallas_call | solution.py:392
  73.3 0.0 copy-start.3
  73.3 0.8 copy-done.3
  74.1 0.0 copy-start.8
  74.1 0.6 copy-done.8
  74.7 72.0 %shard_map.61 = (f32[96,256]{1,0:T(8,128)S(1)}, f32[96,96]{1,0:T(8,128)S(1)}) custom-call(bf16[256,16384]{1,0:T(8,128)(2,1)} %g_hbm.5, bf16[96,256]{1,0:T(8,128)(2,1)S(1)} %copy-done.3, f32[1,256]{1,0:T(1,128)S(1)} %copy-done.8), custom_call_target="tpu_custom_call" | custom-call | flops 805306368 | bytes 8388608 | tf_op jit(solution)/shard_map/pallas_call | solution.py:377
  146.7 0.0 copy-start.1
  146.8 0.6 copy-done.1
  147.4 0.0 copy-start.5
  147.4 0.6 copy-done.5
  148.0 9.8 %shard_map.62 = (f32[96,256]{1,0:T(8,128)}, bf16[96,256]{1,0:T(8,128)(2,1)}) custom-call(f32[96,96]{1,0:T(8,128)} %copy-done.5, f32[96,256]{1,0:T(8,128)} %copy-done.1, f32[1,256]{1,0:T(1,128)} %copy-done.7), custom_call_target="tpu_custom_call" | custom-call | tf_op jit(solution)/shard_map/pallas_call | solution.py:392
  157.8 0.0 copy-start.4
  157.8 0.8 copy-done.4
  158.6 35.3 %shard_map.63 = f32[96,1024]{1,0:T(8,128)S(1)} custom-call(bf16[256,16384]{1,0:T(8,128)(2,1)} %g_hbm.5, bf16[96,256]{1,0:T(8,128)(2,1)S(1)} %copy-done.4), custom_call_target="tpu_custom_call" | custom-call | flops 805306368 | bytes 8388608 | tf_op jit(solution)/shard_map/pallas_call | solution.py:377
  193.9 0.8 bitcast_bitcast_fusion
  (4 shorter events, 0.1 us)
Async XLA Ops:
  0.6 5.0 %copy-start = (f32[8]{0:T(128)S(1)}, f32[8]{0:T(128)}, u32[]{:S(2)}) copy-start(f32[8]{0:T(128)} %param.6) | copy-start | bytes 100
  1.9 4.6 %collective-permute-start = (f32[96,4,128]{2,1,0:T(4,128)S(1)}, f32[96,4,128]{2,1,0:T(4,128)S(1)}, u32[]{:S(2)}, u32[]{:S(2)}) collective-permute-start(f32[96,4,128]{2,1,0:T(4,128)S(1)} %get-tuple-element.16), channel_id=1, source_target_pairs={{0,1},{1,2},{2,3},{3,4},{4,5},{5,6},{6,7},{7,8},{8,9},{9,10},{10,1... | collective-permute-start | bytes 589832 | tf_op jit(solution)/shard_map/ppermute | solution.py:22
  4.3 5.5 %collective-permute-start.1 = (f32[96,4,128]{2,1,0:T(4,128)S(1)}, f32[96,4,128]{2,1,0:T(4,128)S(1)}, u32[]{:S(2)}, u32[]{:S(2)}) collective-permute-start(f32[96,4,128]{2,1,0:T(4,128)S(1)} %get-tuple-element.17), channel_id=1, source_target_pairs={{1,0},{2,1},{3,2},{4,3},{5,4},{6,5},{7,6},{8,7},{9,8},{10,9},{11,1... | collective-permute-start | bytes 589832 | tf_op jit(solution)/shard_map/ppermute | solution.py:23
  6.5 6.2 %copy-start.7 = (f32[1,256]{1,0:T(1,128)}, f32[1,256]{1,0:T(1,128)S(1)}, u32[]{:S(2)}) copy-start(f32[1,256]{1,0:T(1,128)S(1)} %fusion.24.weights_ref) | copy-start | bytes 3076
  62.2 0.6 copy-start.2
  62.9 0.6 copy-start.6
  73.3 0.8 copy-start.3
  74.1 0.6 copy-start.8
  146.7 0.6 copy-start.1
  147.4 0.6 copy-start.5
  157.8 0.8 copy-start.4

commit v4 on v3

--- a/solution.py
+++ b/solution.py
@@ -105,20 +105,22 @@
             over_blocks(place, core, quarter, lambda block: load(block).start())
 
 
-def reduce_scatter(place, load, g_ref, w_ref, acc, wide, outgo, income, sems):
+def reduce_scatter(place, load, g_ref, w_ref, acc, cross, wide, outgo, income, sems):
     n, depth = place.n, acc[0].shape[1]
     width = acc[0].shape[2]
     own = place.bit(0)
     parts = quarters(place)
     fourth = n // 4
 
-    def produce(core, quarter):
+    def produce(core, quarter, target, skip):
         def visit(block):
             load(block).wait()
             columns = pl.ds(pl.multiple_of(block * width, 128), width)
             part = jnp.dot(w_ref[...], g_ref[:, columns], preferred_element_type=jnp.float32)
             for s in range(2):
-                acc[s][place.slot(block, place.orders[s])] = part[s * depth : (s + 1) * depth]
+                target[s][place.slot(block, place.orders[s]) - skip] = part[
+                    s * depth : (s + 1) * depth
+                ].astype(target[s].dtype)
 
         over_blocks(place, core, quarter, visit)
 
@@ -126,21 +128,21 @@
         mine = place.bit(place.orders[s][1])
         at = (1 - mine if piece == 0 else mine) * fourth
         return place.send(
-            acc[s].at[pl.ds((1 - own) * (n // 2) + at, fourth)],
+            cross[s].at[pl.ds(at, fourth)],
             wide[s].at[pl.ds(at, fourth)], 0, sems, place.steps if piece else 0, s,
         )
 
     pieces = [[None, None], [None, None]]
-    produce(1 - own, parts[0])
-    produce(1 - own, parts[1])
+    produce(1 - own, parts[0], cross, (1 - own) * (n // 2))
+    produce(1 - own, parts[1], cross, (1 - own) * (n // 2))
     pieces[0][0] = across(0, 0)
-    produce(1 - own, parts[2])
+    produce(1 - own, parts[2], cross, (1 - own) * (n // 2))
     pieces[1][0] = across(1, 0)
-    produce(1 - own, parts[3])
+    produce(1 - own, parts[3], cross, (1 - own) * (n // 2))
     pieces[0][1] = across(0, 1)
     pieces[1][1] = across(1, 1)
-    produce(own, parts[0])
-    produce(own, parts[1])
+    produce(own, parts[0], acc, 0)
+    produce(own, parts[1], acc, 0)
 
     base = [own * (n // 2), own * (n // 2)]
     copies = [None, None]
@@ -174,9 +176,9 @@
 
         if step == 1:
             out(0)
-            produce(own, parts[2])
+            produce(own, parts[2], acc, 0)
             out(1)
-            produce(own, parts[3])
+            produce(own, parts[3], acc, 0)
             keep(0)
             keep(1)
         else:
@@ -289,26 +291,26 @@
 
 
 def second_kernel(n, scale, g_hbm, w_ref, weights_ref, y_ref, gram_ref, g_ref, loads,
-                  a0, a1, f0, f1, o0, o1, i0, i1, rs_sems,
+                  a0, a1, c0, c1, f0, f1, o0, o1, i0, i1, rs_sems,
                   h0, h1, total, sums, gin, ag_sems, gram_sems):
     place = Place(n)
     load = fetch(g_hbm, g_ref, loads, a0.shape[2])
     start_loads(place, load)
     place.greet()
-    results = reduce_scatter(place, load, g_ref, w_ref, (a0, a1), (f0, f1), (o0, o1), (i0, i1), rs_sems)
+    results = reduce_scatter(place, load, g_ref, w_ref, (a0, a1), (c0, c1), (f0, f1), (o0, o1), (i0, i1), rs_sems)
     for s, held in enumerate((h0, h1)):
         held[place.slot(place.me, place.orders[s])] = (results[s] * scale).astype(jnp.bfloat16)
     gather_product(place, g_ref, (h0, h1), total, ag_sems)
     finish(place, weights_ref, y_ref, gram_ref, total, sums, gin, gram_sems)
 
 
-def last_kernel(n, scale, g_hbm, w_ref, out_ref, g_ref, loads, a0, a1, f0, f1, o0, o1, i0, i1, rs_sems):
+def last_kernel(n, scale, g_hbm, w_ref, out_ref, g_ref, loads, a0, a1, c0, c1, f0, f1, o0, o1, i0, i1, rs_sems):
     place = Place(n)
     depth, width = a0.shape[1:]
     load = fetch(g_hbm, g_ref, loads, width)
     start_loads(place, load)
     place.greet()
-    results = reduce_scatter(place, load, g_ref, w_ref, (a0, a1), (f0, f1), (o0, o1), (i0, i1), rs_sems)
+    results = reduce_scatter(place, load, g_ref, w_ref, (a0, a1), (c0, c1), (f0, f1), (o0, o1), (i0, i1), rs_sems)
     for s in range(2):
         out_ref[s * depth : (s + 1) * depth] = results[s] * scale
 
@@ -355,8 +357,7 @@
 
     scatter_scratch = (
         [pltpu.VMEM((n, depth, width), f32)] * 2
-        + [pltpu.VMEM((n // 2, depth, width), f32)] * 2
-        + [pltpu.VMEM((n // 2, depth, width), bf16)] * 4
+        + [pltpu.VMEM((n // 2, depth, width), bf16)] * 8
         + [pltpu.SemaphoreType.DMA((2, steps + 1, 2))]
     )
     gather_scratch = [pltpu.VMEM((n, depth, width), bf16)] * 2 + [

time: 195 us -> 188 us (0.964)
  Pallas kernels: 176 us -> 169 us
    pallas_call x3, Pallas kernels: 157 us -> 149 us  [call(): pl.pallas_call(kernel, out_shape=shapes, in_specs=[pl.BlockSpec(memory_sp...]
where the time goes in v4:
time: 188 us; the launch traced here: 187 us
  Pallas kernels  169 us (90%)
  local copies, waits for them, and re-layouts  6.78 us (4%)
  starting transfers between devices  3.66 us (2%)
  waiting for transfers between devices  3.19 us (2%)
  other arithmetic  2.91 us (2%)
    pallas_call x3, Pallas kernels, call(): pl.pallas_call(kernel, out_shape=shapes, in_specs=[pl.BlockSpec(memory_sp...  149 us
    pallas_call x2, Pallas kernels, orthonormal(): pl.pallas_call(functools.partial(orthonormal_kernel, float(total_rows)),...  19.7 us
    unnamed x19, local copies, waits for them, and re-layouts  4.77 us
  transfers between devices with their start and end apart: 2, of which 1 were waited for; matrix products, arithmetic and copies ran while one was open for 0% of the time, Pallas kernels for 0%

profile of v4, /device:TPU:0, one launch (start us, length us, event | category | flops | bytes accessed | tf_op | source)
XLA Modules:
  0.0 187.3 jit_solution(13812572030203254265)
XLA Ops:
  0.6 0.0 copy-start
  0.6 1.2 fusion.27
  1.9 2.4 %collective-permute-start = (f32[96,4,128]{2,1,0:T(4,128)S(1)}, f32[96,4,128]{2,1,0:T(4,128)S(1)}, u32[]{:S(2)}, u32[]{:S(2)}) collective-permute-start(f32[96,4,128]{2,1,0:T(4,128)S(1)} %get-tuple-element.16), channel_id=1, source_target_pairs={{0,1},{1,2},{2,3},{3,4},{4,5},{5,6},{6,7},{7,8},{8,9},{9,10},{10,1... | collective-permute-start | bytes 589832 | tf_op jit(solution)/shard_map/ppermute | solution.py:22
  4.3 1.3 collective-permute-start.1
  5.6 0.0 copy-done
  5.6 0.9 fusion.24.weights_ref
  6.5 0.0 copy-start.7
  6.5 0.0 collective-permute-done
  6.6 3.2 %collective-permute-done.1 = f32[96,4,128]{2,1,0:T(4,128)S(1)} collective-permute-done((f32[96,4,128]{2,1,0:T(4,128)S(1)}, f32[96,4,128]{2,1,0:T(4,128)S(1)}, u32[]{:S(2)}, u32[]{:S(2)}) %collective-permute-start.1) | collective-permute-done | bytes 196640 | tf_op jit(solution)/shard_map/ppermute | solution.py:23
  9.7 1.1 pad_maximum_fusion
  10.9 0.5 fusion.5
  11.4 0.5 fusion.11
  11.9 0.5 fusion.17
  12.4 0.3 fusion.23
  12.7 0.0 copy-done.7
  12.7 49.5 %shard_map.59 = (f32[96,256]{1,0:T(8,128)S(1)}, f32[96,96]{1,0:T(8,128)S(1)}) custom-call(bf16[256,16384]{1,0:T(8,128)(2,1)} %g_hbm.5, bf16[96,1024]{1,0:T(8,128)(2,1)S(1)} %bitcast.16, f32[1,256]{1,0:T(1,128)S(1)} %fusion.24.weights_ref), custom_call_target="tpu_custom_call" | custom-call | flops 805306368 | bytes 8388608 | tf_op jit(solution)/shard_map/pallas_call | solution.py:378
  62.2 0.0 copy-start.2
  62.2 0.6 copy-done.2
  62.9 0.0 copy-start.6
  62.9 0.6 copy-done.6
  63.5 9.8 %shard_map.60 = (f32[96,256]{1,0:T(8,128)}, bf16[96,256]{1,0:T(8,128)(2,1)}) custom-call(f32[96,96]{1,0:T(8,128)} %copy-done.6, f32[96,256]{1,0:T(8,128)} %copy-done.2, f32[1,256]{1,0:T(1,128)} %copy-done.7), custom_call_target="tpu_custom_call" | custom-call | tf_op jit(solution)/shard_map/pallas_call | solution.py:393
  73.3 0.0 copy-start.3
  73.3 0.8 copy-done.3
  74.1 0.0 copy-start.8
  74.1 0.6 copy-done.8
  74.7 70.8 %shard_map.61 = (f32[96,256]{1,0:T(8,128)S(1)}, f32[96,96]{1,0:T(8,128)S(1)}) custom-call(bf16[256,16384]{1,0:T(8,128)(2,1)} %g_hbm.5, bf16[96,256]{1,0:T(8,128)(2,1)S(1)} %copy-done.3, f32[1,256]{1,0:T(1,128)S(1)} %copy-done.8), custom_call_target="tpu_custom_call" | custom-call | flops 805306368 | bytes 8388608 | tf_op jit(solution)/shard_map/pallas_call | solution.py:378
  145.5 0.0 copy-start.1
  145.5 0.6 copy-done.1
  146.2 0.0 copy-start.5
  146.2 0.6 copy-done.5
  146.8 9.8 %shard_map.62 = (f32[96,256]{1,0:T(8,128)}, bf16[96,256]{1,0:T(8,128)(2,1)}) custom-call(f32[96,96]{1,0:T(8,128)} %copy-done.5, f32[96,256]{1,0:T(8,128)} %copy-done.1, f32[1,256]{1,0:T(1,128)} %copy-done.7), custom_call_target="tpu_custom_call" | custom-call | tf_op jit(solution)/shard_map/pallas_call | solution.py:393
  156.6 0.0 copy-start.4
  156.6 0.8 copy-done.4
  157.4 29.1 %shard_map.63 = f32[96,1024]{1,0:T(8,128)S(1)} custom-call(bf16[256,16384]{1,0:T(8,128)(2,1)} %g_hbm.5, bf16[96,256]{1,0:T(8,128)(2,1)S(1)} %copy-done.4), custom_call_target="tpu_custom_call" | custom-call | flops 805306368 | bytes 8388608 | tf_op jit(solution)/shard_map/pallas_call | solution.py:378
  186.6 0.8 bitcast_bitcast_fusion
  (4 shorter events, 0.1 us)
Async XLA Ops:
  0.6 5.0 %copy-start = (f32[8]{0:T(128)S(1)}, f32[8]{0:T(128)}, u32[]{:S(2)}) copy-start(f32[8]{0:T(128)} %param.6) | copy-start | bytes 100
  1.9 4.6 %collective-permute-start = (f32[96,4,128]{2,1,0:T(4,128)S(1)}, f32[96,4,128]{2,1,0:T(4,128)S(1)}, u32[]{:S(2)}, u32[]{:S(2)}) collective-permute-start(f32[96,4,128]{2,1,0:T(4,128)S(1)} %get-tuple-element.16), channel_id=1, source_target_pairs={{0,1},{1,2},{2,3},{3,4},{4,5},{5,6},{6,7},{7,8},{8,9},{9,10},{10,1... | collective-permute-start | bytes 589832 | tf_op jit(solution)/shard_map/ppermute | solution.py:22
  4.3 5.5 %collective-permute-start.1 = (f32[96,4,128]{2,1,0:T(4,128)S(1)}, f32[96,4,128]{2,1,0:T(4,128)S(1)}, u32[]{:S(2)}, u32[]{:S(2)}) collective-permute-start(f32[96,4,128]{2,1,0:T(4,128)S(1)} %get-tuple-element.17), channel_id=1, source_target_pairs={{1,0},{2,1},{3,2},{4,3},{5,4},{6,5},{7,6},{8,7},{9,8},{10,9},{11,1... | collective-permute-start | bytes 589832 | tf_op jit(solution)/shard_map/ppermute | solution.py:23
  6.5 6.2 %copy-start.7 = (f32[1,256]{1,0:T(1,128)}, f32[1,256]{1,0:T(1,128)S(1)}, u32[]{:S(2)}) copy-start(f32[1,256]{1,0:T(1,128)S(1)} %fusion.24.weights_ref) | copy-start | bytes 3076
  62.2 0.6 copy-start.2
  62.9 0.6 copy-start.6
  73.3 0.8 copy-start.3
  74.1 0.6 copy-start.8
  145.5 0.6 copy-start.1
  146.2 0.6 copy-start.5
  156.6 0.8 copy-start.4
